TPU v7x, 32 devices: a whole 2x2x4 slice. The times are simulated.
32 devices in a mesh: dp: 16 (over z, y, x), feat: 2 (over core).
Axes of the slice: x: 2, y: 2, z: 4, core: 2. Of those that a mesh axis runs over, the one named last changes fastest.
Arguments:
- inputs: float32 [20480, 640], P('dp', 'feat'), may hold values from -6 to 6
- encoder: bfloat16 [20480, 640], P('dp', 'feat'), may hold values from -6 to 6
- output_grad: float32 [20480, 640], P('dp', 'feat'), may hold values from -6 to 6
- target_lengths: int32 [32, 24], P(('dp', 'feat')), may hold values from 0 to 256, as said below
- source_lengths: int32 [32, 24], P(('dp', 'feat')), may hold values from 0 to 256, as said below
- gains: float32 [3, 640], P(None, 'feat'), may hold values from 0.5 to 1.5
- shifts: float32 [3, 640], P(None, 'feat'), may hold values from -2 to 2
- self_inproj: bfloat16 [640, 1920], replicated, may hold values from -0.25 to 0.25
- self_outproj: bfloat16 [640, 640], replicated, may hold values from -1 to 1
- cross_query: bfloat16 [640, 640], replicated, may hold values from -0.25 to 0.25
- cross_keyvalue: bfloat16 [640, 1280], replicated, may hold values from -0.25 to 0.25
- cross_outproj: bfloat16 [640, 640], replicated, may hold values from -1 to 1
- ffn_expand: bfloat16 [640, 3072], replicated, may hold values from -0.25 to 0.25
- ffn_reduce: bfloat16 [3072, 640], replicated, may hold values from -0.109375 to 0.109375
Outputs:
- layer_out: float32 [20480, 640], P('dp', 'feat')
- input_grad: float32 [20480, 640], P('dp', 'feat')
- encoder_grad: float32 [20480, 640], P('dp', 'feat')
- gain_grad: float32 [3, 640], P(None, 'feat')
- shift_grad: float32 [3, 640], P(None, 'feat')
- self_inproj_grad: float32 [640, 1920], P('dp', 'feat')
- self_outproj_grad: float32 [640, 640], P('dp', 'feat')
- cross_query_grad: float32 [640, 640], P('dp', 'feat')
- cross_keyvalue_grad: float32 [640, 1280], P('dp', 'feat')
- cross_outproj_grad: float32 [640, 640], P('dp', 'feat')
- ffn_expand_grad: float32 [640, 3072], P('dp', 'feat')
- ffn_reduce_grad: float32 [3072, 640], P('dp', 'feat')
Inputs may be any that keep to these rules, and one draw needn't show every extreme that they name: `target_lengths`: in each bucket the nonzero lengths fill the first slots and zeros the rest; a bucket's lengths sum to 640 or less; in every draw one bucket, chosen from the seed, has a first sentence of 256. `source_lengths`: nonzero exactly where target_lengths is, and at most the target length.
All inputs are finite; a program needn't handle non-finite values.
Results may differ from a plain program's by a relative error of at most 0.017.
Values may be sent and summed in bfloat16 or wider, within the bound.
A program may use at most 192 MiB of HBM per device.

v0:
```python
import math
import jax
import jax.numpy as jnp
from jax import lax
from jax.sharding import PartitionSpec as P

HEADS = 8
EPSILON = 1e-05
MASKED_SCORE = -1e30


def as_sent(array):

    def short(part):
        return part.astype(jnp.bfloat16) if part.dtype == jnp.float32 else part

    return jax.tree.map(short, array)


def inner(left, right):
    return lax.dot_general(
        left, right, (((0,), (0,)), ((), ())), preferred_element_type=jnp.float32
    )


def backward_product(grad, weight):
    return lax.dot_general(
        grad, weight, (((1,), (1,)), ((), ())), preferred_element_type=jnp.float32
    )


def smooth_gate(values):
    return jax.nn.gelu(values, approximate=True)


def row_sums(first, second):
    return (first, second)


def to_tokens(parts):
    return parts


def to_features(parts):
    return parts


def gather_rows(part):
    return lax.all_to_all(part, "feat", split_axis=0, concat_axis=1, tiled=True)


def spread_rows(part):
    return lax.all_to_all(part, "feat", split_axis=1, concat_axis=0, tiled=True)


def norm_forward(values, gain, shift):
    width = values.shape[1]
    total, squares = row_sums(jnp.sum(values, axis=1), jnp.sum(values * values, axis=1))
    center = total / width
    reciprocal = lax.rsqrt(squares / width - center * center + EPSILON)
    normed = (values - center[:, None]) * reciprocal[:, None]
    return (normed, reciprocal, (normed * gain + shift).astype(jnp.bfloat16))


def norm_backward(grad_normed, normed, reciprocal, gain):
    width = normed.shape[1]
    grad_value = grad_normed.astype(jnp.float32)
    scaled = grad_value * gain
    first, second = row_sums(jnp.sum(scaled, axis=1), jnp.sum(scaled * normed, axis=1))
    grad_input = reciprocal[:, None] * (
        scaled - first[:, None] / width - normed * (second[:, None] / width)
    )
    return (grad_input, jnp.sum(grad_value * normed, axis=0), jnp.sum(grad_value, axis=0))


def sentence_rows(lengths, count):
    slots = jnp.arange(lengths.shape[1], dtype=jnp.int32)
    ends = jnp.sum(
        jnp.where(slots[:, None] <= slots[None, :], lengths[0][:, None], 0), axis=0, dtype=jnp.int32
    )
    positions = jnp.arange(count, dtype=jnp.int32)
    sentence = jnp.sum(
        (ends[None, :] <= positions[:, None]).astype(jnp.int32), axis=1, dtype=jnp.int32
    )
    return (sentence, positions < ends[-1])


def split_heads(values):
    return values.reshape(values.shape[0], HEADS, values.shape[1] // HEADS)


def head_scores(queries, keys, allowed):
    head_size = queries.shape[1] // HEADS
    scores = jnp.einsum(
        "qhd,khd->hqk", split_heads(queries), split_heads(keys), preferred_element_type=jnp.float32
    ) * (1.0 / math.sqrt(head_size))
    return jnp.where(allowed[None, :, :], scores, MASKED_SCORE)


def attend_forward(queries, keys, values, allowed):
    scores = head_scores(queries, keys, allowed)
    largest = jnp.max(scores, axis=-1, keepdims=True)
    expo = jnp.exp(scores - largest)
    total = jnp.sum(expo, axis=-1, keepdims=True)
    weights = expo / total
    mixed = jnp.einsum(
        "hqk,khd->qhd",
        weights.astype(jnp.bfloat16),
        split_heads(values),
        preferred_element_type=jnp.float32,
    )
    log_total = largest[..., 0] + jnp.log(total[..., 0])
    return (mixed.reshape(queries.shape).astype(jnp.bfloat16), log_total)


def attend_backward(queries, keys, values, allowed, log_total, grad_mixed):
    head_size = queries.shape[1] // HEADS
    scale = 1.0 / math.sqrt(head_size)
    weights = jnp.exp(head_scores(queries, keys, allowed) - log_total[..., None])
    grad_heads = split_heads(grad_mixed)
    grad_weights = jnp.einsum(
        "qhd,khd->hqk", grad_heads, split_heads(values), preferred_element_type=jnp.float32
    )
    grad_values = jnp.einsum(
        "hqk,qhd->khd", weights.astype(jnp.bfloat16), grad_heads, preferred_element_type=jnp.float32
    )
    centre = jnp.sum(weights * grad_weights, axis=-1, keepdims=True)
    grad_scores = (weights * (grad_weights - centre)).astype(jnp.bfloat16)
    grad_queries = (
        jnp.einsum(
            "hqk,khd->qhd", grad_scores, split_heads(keys), preferred_element_type=jnp.float32
        )
        * scale
    )
    grad_keys = (
        jnp.einsum(
            "hqk,qhd->khd", grad_scores, split_heads(queries), preferred_element_type=jnp.float32
        )
        * scale
    )
    return (
        grad_queries.reshape(queries.shape),
        grad_keys.reshape(keys.shape),
        grad_values.reshape(values.shape),
    )


def masked_rows(grad, valid):
    return jnp.where(valid[:, None], grad, jnp.zeros_like(grad))


def per_device(
    inputs,
    encoder,
    output_grad,
    target_lengths,
    source_lengths,
    gains,
    shifts,
    self_inproj,
    self_outproj,
    cross_query,
    cross_keyvalue,
    cross_outproj,
    ffn_expand,
    ffn_reduce,
):
    inputs = gather_rows(inputs)
    encoder = gather_rows(encoder)
    output_grad = gather_rows(output_grad)
    gains = lax.all_gather(gains, "feat", axis=1, tiled=True)
    shifts = lax.all_gather(shifts, "feat", axis=1, tiled=True)
    count = inputs.shape[0]
    width = self_outproj.shape[0]
    target_seg, target_valid = sentence_rows(target_lengths, count)
    source_seg, source_valid = sentence_rows(source_lengths, count)
    positions = jnp.arange(count, dtype=jnp.int32)
    keep = target_valid.astype(jnp.float32)[:, None]
    self_mask = (target_seg[:, None] == target_seg[None, :]) & (
        positions[None, :] <= positions[:, None]
    )
    self_mask = self_mask & target_valid[:, None] & target_valid[None, :]
    cross_mask = (
        (target_seg[:, None] == source_seg[None, :]) & target_valid[:, None] & source_valid[None, :]
    )
    normed_one, recip_one, normed_cols = norm_forward(inputs, gains[0], shifts[0])
    (normed1,) = to_tokens((normed_cols,))
    projected = jnp.dot(normed1, self_inproj, preferred_element_type=jnp.float32).astype(
        jnp.bfloat16
    )
    queries = projected[:, :width]
    keys = projected[:, width : 2 * width]
    values = projected[:, 2 * width :]
    attended1, log_one = attend_forward(queries, keys, values, self_mask)
    branch = (jnp.dot(attended1, self_outproj, preferred_element_type=jnp.float32) * keep).astype(
        jnp.bfloat16
    )
    (branch_cols,) = to_features((branch,))
    mid_one = inputs + branch_cols.astype(jnp.float32)
    normed_two, recip_two, normed_cols = norm_forward(mid_one, gains[1], shifts[1])
    normed2, source_rows = to_tokens((normed_cols, encoder))
    cross_queries = jnp.dot(normed2, cross_query, preferred_element_type=jnp.float32).astype(
        jnp.bfloat16
    )
    memory = jnp.dot(source_rows, cross_keyvalue, preferred_element_type=jnp.float32).astype(
        jnp.bfloat16
    )
    attended2, log_two = attend_forward(
        cross_queries, memory[:, :width], memory[:, width:], cross_mask
    )
    branch = (jnp.dot(attended2, cross_outproj, preferred_element_type=jnp.float32) * keep).astype(
        jnp.bfloat16
    )
    (branch_cols,) = to_features((branch,))
    mid_two = mid_one + branch_cols.astype(jnp.float32)
    normed_three, recip_three, normed_cols = norm_forward(mid_two, gains[2], shifts[2])
    (normed3,) = to_tokens((normed_cols,))
    expanded = jnp.dot(normed3, ffn_expand, preferred_element_type=jnp.float32).astype(jnp.bfloat16)
    gated, gate_pull = jax.vjp(smooth_gate, expanded.astype(jnp.float32))
    activated = gated.astype(jnp.bfloat16)
    branch = (jnp.dot(activated, ffn_reduce, preferred_element_type=jnp.float32) * keep).astype(
        jnp.bfloat16
    )
    (branch_cols,) = to_features((branch,))
    layer_out = mid_two + branch_cols.astype(jnp.float32)
    (grad_branch,) = to_tokens((output_grad.astype(jnp.bfloat16),))
    grad_branch = masked_rows(grad_branch, target_valid)
    reduce_grad = inner(activated, grad_branch)
    grad_act = backward_product(grad_branch, ffn_reduce)
    (grad_pre,) = gate_pull(grad_act)
    grad_expanded = grad_pre.astype(jnp.bfloat16)
    expand_grad = inner(normed3, grad_expanded)
    grad_normed = backward_product(grad_expanded, ffn_expand).astype(jnp.bfloat16)
    (grad_cols,) = to_features((grad_normed,))
    part_three, gain_three, shift_three = norm_backward(
        grad_cols, normed_three, recip_three, gains[2]
    )
    grad_mid_two = output_grad + part_three
    (grad_branch,) = to_tokens((grad_mid_two.astype(jnp.bfloat16),))
    grad_branch = masked_rows(grad_branch, target_valid)
    cross_out_grad = inner(attended2, grad_branch)
    grad_attended = backward_product(grad_branch, cross_outproj).astype(jnp.bfloat16)
    grad_cq, grad_ck, grad_cv = attend_backward(
        cross_queries, memory[:, :width], memory[:, width:], cross_mask, log_two, grad_attended
    )
    grad_cq = grad_cq.astype(jnp.bfloat16)
    grad_memory = jnp.concatenate([grad_ck, grad_cv], axis=1).astype(jnp.bfloat16)
    cross_query_grad = inner(normed2, grad_cq)
    cross_kv_grad = inner(source_rows, grad_memory)
    grad_normed = backward_product(grad_cq, cross_query).astype(jnp.bfloat16)
    grad_source = backward_product(grad_memory, cross_keyvalue).astype(jnp.bfloat16)
    grad_cols, grad_source_cols = to_features((grad_normed, grad_source))
    part_two, gain_two, shift_two = norm_backward(grad_cols, normed_two, recip_two, gains[1])
    grad_mid_one = grad_mid_two + part_two
    (grad_branch,) = to_tokens((grad_mid_one.astype(jnp.bfloat16),))
    grad_branch = masked_rows(grad_branch, target_valid)
    self_out_grad = inner(attended1, grad_branch)
    grad_attended = backward_product(grad_branch, self_outproj).astype(jnp.bfloat16)
    grad_q, grad_k, grad_v = attend_backward(
        queries, keys, values, self_mask, log_one, grad_attended
    )
    grad_projected = jnp.concatenate([grad_q, grad_k, grad_v], axis=1).astype(jnp.bfloat16)
    self_in_grad = inner(normed1, grad_projected)
    grad_normed = backward_product(grad_projected, self_inproj).astype(jnp.bfloat16)
    (grad_cols,) = to_features((grad_normed,))
    part_one, gain_one, shift_one = norm_backward(grad_cols, normed_one, recip_one, gains[0])
    input_grad = grad_mid_one + part_one
    gain_local = jnp.stack([gain_one, gain_two, gain_three], axis=0)
    shift_local = jnp.stack([shift_one, shift_two, shift_three], axis=0)
    vectors = lax.psum(jnp.concatenate([gain_local, shift_local], axis=0), ("dp", "feat"))
    half = vectors.shape[1] // lax.axis_size("feat")
    vectors = lax.dynamic_slice_in_dim(vectors, lax.axis_index("feat") * half, half, axis=1)
    gain_grad, shift_grad = (vectors[:3], vectors[3:])
    weight_terms = (
        self_in_grad,
        self_out_grad,
        cross_query_grad,
        cross_kv_grad,
        cross_out_grad,
        expand_grad,
        reduce_grad,
    )
    summed = []
    for term in weight_terms:
        pair = lax.psum_scatter(term.astype(jnp.bfloat16), "feat", scatter_dimension=1, tiled=True)
        summed.append(
            lax.psum_scatter(pair, "dp", scatter_dimension=0, tiled=True).astype(jnp.float32)
        )
    return (
        spread_rows(layer_out),
        spread_rows(input_grad),
        spread_rows(grad_source_cols).astype(jnp.float32),
        gain_grad,
        shift_grad,
        *summed,
    )


def solution(mesh):
    in_specs = (
        P("dp", "feat"),
        P("dp", "feat"),
        P("dp", "feat"),
        P(("dp", "feat"), None),
        P(("dp", "feat"), None),
        P(None, "feat"),
        P(None, "feat"),
        P(),
        P(),
        P(),
        P(),
        P(),
        P(),
        P(),
    )
    out_specs = (
        P("dp", "feat"),
        P("dp", "feat"),
        P("dp", "feat"),
        P(None, "feat"),
        P(None, "feat"),
        P("dp", "feat"),
        P("dp", "feat"),
        P("dp", "feat"),
        P("dp", "feat"),
        P("dp", "feat"),
        P("dp", "feat"),
        P("dp", "feat"),
    )
    return jax.shard_map(
        per_device, mesh=mesh, in_specs=in_specs, out_specs=out_specs, check_vma=False
    )
```

profile of v0, /device:TPU:0, one launch (start us, length us, event | category | flops | bytes accessed | tf_op | source)
XLA Modules:
  0.0 732.3 jit_solution(13034640641992369800)
XLA Ops:
  7.2 2.3 copy.193
  9.5 3.5 all-to-all-start.1
  20.5 2.7 copy.192
  23.2 4.7 all-to-all-start
  27.8 2.9 convolution_convert_fusion.6
  35.3 2.7 copy.191
  38.0 4.7 all-to-all-start.3
  58.6 8.8 %fusion.79 = f32[640,3072]{1,0:T(8,128)} fusion(bf16[640,640]{0,1:T(8,128)(2,1)S(1)} %fusion.60, bf16[3072,640]{1,0:T(8,128)(2,1)} %param.27), kind=kOutput, calls=%fused_computation.178 | convolution fusion | flops 2516582400 | bytes 12615680 | tf_op jit(solution)/shard_map/dot_general | solution.py:27
  68.6 2.5 fusion.77
  72.9 2.9 copy-done.1
  75.8 3.7 fusion.59
  79.5 2.8 fusion.73
  84.1 2.5 fusion.78
  88.7 2.7 copy-done.2
  91.4 3.8 fusion.58
  97.4 12.5 %fusion.7 = (bf16[640,3072]{1,0:T(8,128)(2,1)S(1)}, bf16[640,3072]{1,0:T(8,128)(2,1)}) fusion(f32[640,3072]{1,0:T(8,128)} %fusion.79, bf16[640,3072]{1,0:T(8,128)(2,1)S(1)} %copy-done.50, f32[640,640]{0,1:T(8,128)S(1)} %get-tuple-element.118, f32[640]{0:T(1024)S(1)} %get-tuple-element.91, f32[640]{0:T(1024)S(1)} %get-tuple-element.130, ...), kind=kOutput, calls=%fused_computation.24 | convolution fusion | flops 2561884160 | bytes 21309440 | tf_op jit(solution)/shard_map/dot_general | solution.py:218
  109.9 3.6 fusion.44
  118.6 2.6 convolution_convert_fusion.11
  121.3 12.5 %multiply_reduce_fusion.1 = (f32[8,640]{1,0:T(8,128)S(1)}, f32[8,640,640]{1,2,0:T(8,128)}) fusion(f32[8,640,640]{1,2,0:T(8,128)} %copy-done.2, f32[8,640]{1,0:T(8,128)S(1)} %log_add_fusion.1, bf16[640,8,80]{0,2,1:T(8,128)(2,1)S(1)} %bitcast.172, bf16[640,8,80]{0,2,1:T(8,128)(2,1)} %bitcast.186), kind=kOutput, calls=%fused_computation.9 | convolution fusion | flops 534113280 | bytes 27893760 | tf_op jit(solution)/shard_map/qhd,khd->hqk/dot_general | solution.py:121
  133.8 6.6 multiply_convert_fusion.1
  146.4 3.2 fusion.45
  153.2 5.6 multiply_convert_fusion.2
  158.8 7.3 fusion.52
  167.0 2.8 fusion.22
  170.1 2.4 convolution_convert_fusion.9
  172.5 12.1 %multiply_reduce_fusion = (f32[8,640]{1,0:T(8,128)S(1)}, f32[8,640,640]{1,2,0:T(8,128)}) fusion(f32[8,640,640]{1,2,0:T(8,128)} %copy-done.1, f32[8,640]{1,0:T(8,128)S(1)} %log_add_fusion, bf16[640,8,80]{0,2,1:T(8,128)(2,1)S(1)} %bitcast.174, bf16[640,8,80]{0,2,1:T(8,128)(2,1)S(1)} %bitcast.184), kind=kOutput, calls=%fused_computation.6 | convolution fusion | flops 534113280 | bytes 27893760 | tf_op jit(solution)/shard_map/qhd,khd->hqk/dot_general | solution.py:121
  185.6 6.6 multiply_convert_fusion
  198.9 3.9 convolution_convert_fusion.3
  204.0 7.4 %convolution_convert_fusion = bf16[3072,640]{0,1:T(8,128)(2,1)} fusion(bf16[640,640]{0,1:T(8,128)(2,1)S(1)} %copy-done.34, bf16[640,3072]{1,0:T(8,128)(2,1)} %get-tuple-element.120), kind=kOutput, calls=%fused_computation.37 | convolution fusion | flops 2538209280 | bytes 8683520 | tf_op jit(solution)/shard_map/dot_general | solution.py:21
  211.5 8.4 %convolution_convert_fusion.1 = bf16[640,3072]{1,0:T(8,128)(2,1)} fusion(bf16[640,3072]{1,0:T(8,128)(2,1)} %copy-done.55, f32[640,640]{0,1:T(8,128)} %copy-done.18, f32[640]{0:T(1024)S(1)} %get-tuple-element.91, f32[640]{0:T(1024)S(1)} %get-tuple-element.130, f32[640]{0:T(1024)S(1)} %get-tuple-element.108, f32[640]{0:T(1024)S(1)} %get-tuple-element.107), kind=kOutput, calls=%fused_computation.38 | convolution fusion | flops 2520596480 | bytes 9512960 | tf_op jit(solution)/shard_map/dot_general | solution.py:21
  220.7 2.5 copy.170
  223.4 8.2 %reduce-scatter.33.cloned.1.call-done = bf16[3072,320]{0,1:T(8,128)(2,1)} async-done(((bf16[3072,640]{0,1:T(8,128)(2,1)}), bf16[3072,320]{0,1:T(8,128)(2,1)}) %reduce-scatter.33.cloned.1.call-update) | async-done | bytes 1966096 | tf_op jit(solution)/shard_map/reduce_scatter | solution.py:285
  231.6 4.1 copy.180
  235.8 11.1 %reduce-scatter.29.cloned.1.call-done = bf16[640,1536]{1,0:T(8,128)(2,1)} async-done(((bf16[640,3072]{1,0:T(8,128)(2,1)}), bf16[640,1536]{1,0:T(8,128)(2,1)}) %reduce-scatter.29.cloned.1.call-update) | async-done | bytes 1966096 | tf_op jit(solution)/shard_map/reduce_scatter | solution.py:285
  246.9 8.8 %convert_add_fusion.1 = f32[640,640]{0,1:T(8,128)} fusion(f32[640,640]{0,1:T(8,128)} %copy-done.18, bf16[3072,640]{1,0:T(8,128)(2,1)} %param.27, f32[640]{0:T(1024)S(1)} %fusion.61, bf16[640,3072]{1,0:T(8,128)(2,1)} %get-tuple-element.120), kind=kOutput, calls=%fused_computation.93 | convolution fusion | flops 2537881600 | bytes 11143680 | tf_op jit(solution)/shard_map/dot_general | solution.py:221
  255.8 4.8 all-to-all-start.2
  260.6 4.1 convolution_convert_fusion.7
  264.7 4.0 all-to-all-start.5
  268.7 2.9 copy.185
  271.6 4.0 fusion.46
  275.7 3.2 fusion.34
  278.9 4.7 all-to-all-start.4
  286.2 2.7 copy.186
  290.2 40.8 %psum.7 = f32[6,640]{1,0:T(8,128)S(1)} all-reduce(f32[6,640]{1,0:T(8,128)S(1)} %concatenate.13), channel_id=1, replica_groups=mesh['dp'=16,'feat'=2] {'dp','feat'}, use_global_device_ids=true, to_apply=%region_28.29 | all-reduce | flops 3840 | bytes 30720 | tf_op jit(solution)/shard_map/psum | solution.py:270
  331.7 50.3 %all-reduce.7.cloned.1.call-done = (bf16[640,320]{0,1:T(8,128)(2,1)}, bf16[640,320]{0,1:T(8,128)(2,1)}, bf16[640,640]{0,1:T(8,128)(2,1)}, bf16[640,320]{0,1:T(8,128)(2,1)}) async-done(((bf16[640,320]{0,1:T(8,128)(2,1)}, bf16[640,320]{0,1:T(8,128)(2,1)}, bf16[640,640]{0,1:T(8,128)(2,1)}, bf16[640,320]{0,1:T(8,128)(2,1)}), (bf16[640,320]{0,1:T(8,128)(2,1)}, bf16[640,320]{0,1:T(8,128)(2,1)}, ...) | async-done | bytes 2048016
  389.1 73.2 %reduce-scatter.35.cloned.1.call-done = bf16[40,960]{1,0:T(8,128)(2,1)} async-done(((bf16[640,960]{1,0:T(8,128)(2,1)}), bf16[40,960]{1,0:T(8,128)(2,1)}) %reduce-scatter.35.cloned.1.call-update) | async-done | bytes 76816
  464.1 127.7 %reduce-scatter.37.cloned.1.call-done = bf16[192,320]{1,0:T(8,128)(2,1)} async-done(((bf16[3072,320]{1,0:T(8,128)(2,1)}), bf16[192,320]{1,0:T(8,128)(2,1)}) %reduce-scatter.37.cloned.1.call-update) | async-done | bytes 122896
  593.7 129.9 %reduce-scatter.31.cloned.1.call-done = bf16[40,1536]{1,0:T(8,128)(2,1)} async-done(((bf16[640,1536]{1,0:T(8,128)(2,1)}), bf16[40,1536]{1,0:T(8,128)(2,1)}) %reduce-scatter.31.cloned.1.call-update) | async-done | bytes 122896 | tf_op jit(solution)/shard_map/reduce_scatter | solution.py:287
  (237 shorter events, 78.4 us)
Async XLA Ops:
  7.2 40.5 %copy-start = (bf16[640,1920]{1,0:T(8,128)(2,1)S(1)}, bf16[640,1920]{1,0:T(8,128)(2,1)}, u32[]{:S(2)}) copy-start(bf16[640,1920]{1,0:T(8,128)(2,1)} %param.21) | copy-start | bytes 7372804
  7.2 5.8 copy-start.52
  7.2 7.8 %copy-start.53 = (s32[1,24]{1,0:T(1,128)S(1)}, s32[1,24]{1,0:T(1,128)}, u32[]{:S(2)}) copy-start(s32[1,24]{1,0:T(1,128)} %param.18) | copy-start | bytes 292
  7.2 9.3 %copy-start.48 = (f32[3,320]{1,0:T(4,128)S(1)}, f32[3,320]{1,0:T(4,128)}, u32[]{:S(2)}) copy-start(f32[3,320]{1,0:T(4,128)} %param.19) | copy-start | bytes 11524
  7.2 11.3 %copy-start.49 = (f32[3,320]{1,0:T(4,128)S(1)}, f32[3,320]{1,0:T(4,128)}, u32[]{:S(2)}) copy-start(f32[3,320]{1,0:T(4,128)} %param.20) | copy-start | bytes 11524
  9.5 13.7 %all-to-all-start.1 = ((bf16[2,640,320]{1,2,0:T(8,128)(2,1)}), bf16[2,640,320]{1,2,0:T(8,128)(2,1)S(1)}, u32[]{:S(2)}, u32[]{:S(2)}) async-start(bf16[2,640,320]{1,2,0:T(8,128)(2,1)} %bitcast.161), calls=%async_computation.1 | async-start | bytes 1638400 | tf_op jit(solution)/shard_map/all_to_all | solution.py:49
  23.2 4.7 copy-start.29
  23.2 14.9 %all-to-all-start = ((f32[2,640,320]{1,2,0:T(8,128)}), f32[2,640,320]{1,2,0:T(8,128)}, u32[]{:S(2)}, u32[]{:S(2)}) async-start(f32[2,640,320]{1,2,0:T(8,128)} %bitcast.177), calls=%async_computation | async-start | bytes 3276800 | tf_op jit(solution)/shard_map/all_to_all | solution.py:49
  38.0 8.0 %copy-start.42 = (f32[640]{0:T(1024)}, f32[640]{0:T(1024)S(1)}, u32[]{:S(2)}) copy-start(f32[640]{0:T(1024)S(1)} %get-tuple-element.128) | copy-start | bytes 7684
  38.0 19.0 %all-to-all-start.3 = ((f32[2,640,320]{1,2,0:T(8,128)}), f32[2,640,320]{1,2,0:T(8,128)}, u32[]{:S(2)}, u32[]{:S(2)}) async-start(f32[2,640,320]{1,2,0:T(8,128)} %bitcast.176), calls=%async_computation.3 | async-start | bytes 3276800 | tf_op jit(solution)/shard_map/all_to_all | solution.py:49
  42.7 177.3 %reduce-scatter.27.cloned.1.call-start = ((), (), s32[]{:S(2)}) async-start(), calls=%async_computation.20 | async-start | bytes 1228800 | tf_op jit(solution)/shard_map/reduce_scatter | solution.py:285
  45.9 4.0 copy-start.44
  58.6 8.8 %copy-start.33 = (bf16[640,640]{0,1:T(8,128)(2,1)}, bf16[640,640]{0,1:T(8,128)(2,1)S(1)}, u32[]{:S(2)}) copy-start(bf16[640,640]{0,1:T(8,128)(2,1)S(1)} %fusion.60) | copy-start | bytes 2457604
  58.6 10.0 %copy-start.12 = (bf16[640,640]{0,1:T(8,128)(2,1)S(1)}, bf16[640,640]{0,1:T(8,128)(2,1)}, u32[]{:S(2)}) copy-start(bf16[640,640]{0,1:T(8,128)(2,1)} %copy.140) | copy-start | bytes 2457604
  58.6 10.0 %copy-start.16 = (bf16[640,640]{0,1:T(8,128)(2,1)S(1)}, bf16[640,640]{0,1:T(8,128)(2,1)}, u32[]{:S(2)}) copy-start(bf16[640,640]{0,1:T(8,128)(2,1)} %copy.139) | copy-start | bytes 2457604
  71.1 4.7 copy-start.1
  86.7 4.7 copy-start.2
  96.4 17.2 %copy-start.18 = (f32[640,640]{0,1:T(8,128)}, f32[640,640]{0,1:T(8,128)S(1)}, u32[]{:S(2)}) copy-start(f32[640,640]{0,1:T(8,128)S(1)} %get-tuple-element.118) | copy-start | bytes 4915204
  118.6 101.5 %reduce-scatter.23.cloned.1.call-start = ((), (), s32[]{:S(2)}) async-start(), calls=%async_computation.18 | async-start | bytes 1228800 | tf_op jit(solution)/shard_map/reduce_scatter | solution.py:285
  121.2 12.6 %slice-start.4 = ((s8[13107200]{0:T(1024)(128)(4,1)}), s8[4194304]{0:T(1024)(128)(4,1)S(1)}, s32[]{:S(2)}) async-start(s8[13107200]{0:T(1024)(128)(4,1)} %bitcast.164), calls=%async_computation.31 | async-start | bytes 8388608
  121.2 12.5 %slice-start.5 = ((s8[13107200]{0:T(1024)(128)(4,1)}), s8[4194304]{0:T(1024)(128)(4,1)S(1)}, s32[]{:S(2)}) async-start(s8[13107200]{0:T(1024)(128)(4,1)} %bitcast.164), calls=%async_computation.32 | async-start | bytes 8388608
  121.2 12.5 %slice-start.6 = ((s8[13107200]{0:T(1024)(128)(4,1)}), s8[4194304]{0:T(1024)(128)(4,1)S(1)}, s32[]{:S(2)}) async-start(s8[13107200]{0:T(1024)(128)(4,1)} %bitcast.164), calls=%async_computation.33 | async-start | bytes 8388608
  121.2 12.5 %slice-start.7 = ((s8[13107200]{0:T(1024)(128)(4,1)}), s8[524288]{0:T(1024)(128)(4,1)S(1)}, s32[]{:S(2)}) async-start(s8[13107200]{0:T(1024)(128)(4,1)} %bitcast.164), calls=%async_computation.34 | async-start | bytes 1048576
  133.8 6.6 copy-start.15
  146.1 73.9 %reduce-scatter.21.cloned.1.call-start = ((), (), s32[]{:S(2)}) async-start(), calls=%async_computation.17 | async-start | bytes 1228800 | tf_op jit(solution)/shard_map/reduce_scatter | solution.py:285
  153.1 66.9 %reduce-scatter.25.cloned.1.call-start = ((), (), s32[]{:S(2)}) async-start(), calls=%async_computation.19 | async-start | bytes 2457600 | tf_op jit(solution)/shard_map/reduce_scatter | solution.py:285
  158.8 7.3 copy-start.35
  158.8 8.2 %copy-start.30 = (bf16[2,640,320]{1,2,0:T(8,128)(2,1)S(1)}, bf16[2,640,320]{1,2,0:T(8,128)(2,1)}, u32[]{:S(2)}) copy-start(bf16[2,640,320]{1,2,0:T(8,128)(2,1)} %copy-done.29) | copy-start | bytes 2457604
  169.8 51.0 %reduce-scatter.19.cloned.1.call-start = ((), (), s32[]{:S(2)}) async-start(), calls=%async_computation.16 | async-start | bytes 3686400 | tf_op jit(solution)/shard_map/reduce_scatter | solution.py:285
  172.5 12.1 %slice-start = ((s8[13107200]{0:T(1024)(128)(4,1)}), s8[4194304]{0:T(1024)(128)(4,1)S(1)}, s32[]{:S(2)}) async-start(s8[13107200]{0:T(1024)(128)(4,1)} %bitcast.162), calls=%async_computation.27 | async-start | bytes 8388608
  172.5 12.1 %slice-start.1 = ((s8[13107200]{0:T(1024)(128)(4,1)}), s8[4194304]{0:T(1024)(128)(4,1)S(1)}, s32[]{:S(2)}) async-start(s8[13107200]{0:T(1024)(128)(4,1)} %bitcast.162), calls=%async_computation.28 | async-start | bytes 8388608
  172.5 12.9 %slice-start.2 = ((s8[13107200]{0:T(1024)(128)(4,1)}), s8[4194304]{0:T(1024)(128)(4,1)S(1)}, s32[]{:S(2)}) async-start(s8[13107200]{0:T(1024)(128)(4,1)} %bitcast.162), calls=%async_computation.29 | async-start | bytes 8388608
  172.5 13.1 %slice-start.3 = ((s8[13107200]{0:T(1024)(128)(4,1)}), s8[524288]{0:T(1024)(128)(4,1)S(1)}, s32[]{:S(2)}) async-start(s8[13107200]{0:T(1024)(128)(4,1)} %bitcast.162), calls=%async_computation.30 | async-start | bytes 1048576
  185.6 6.6 copy-start.17
  202.8 28.7 %reduce-scatter.33.cloned.1.call-start = ((), (), s32[]{:S(2)}) async-start(), calls=%async_computation.23 | async-start | bytes 5898240 | tf_op jit(solution)/shard_map/reduce_scatter | solution.py:285
  211.4 35.5 %reduce-scatter.29.cloned.1.call-start = ((), (), s32[]{:S(2)}) async-start(), calls=%async_computation.21 | async-start | bytes 5898240 | tf_op jit(solution)/shard_map/reduce_scatter | solution.py:285
  219.9 162.0 %all-reduce.7.cloned.1.call-start = ((), (), s32[]{:S(2)}) async-start(), calls=%async_computation.26 | async-start | bytes 4096000
  220.7 241.6 %reduce-scatter.35.cloned.1.call-start = ((), (), s32[]{:S(2)}) async-start(), calls=%async_computation.24 | async-start | bytes 1392640
  223.3 368.5 %reduce-scatter.37.cloned.1.call-start = ((), (), s32[]{:S(2)}) async-start(), calls=%async_computation.25 | async-start | bytes 2506752
  235.7 487.9 %reduce-scatter.31.cloned.1.call-start = ((), (), s32[]{:S(2)}) async-start(), calls=%async_computation.22 | async-start | bytes 2088960 | tf_op jit(solution)/shard_map/reduce_scatter | solution.py:287
  255.8 4.8 copy-start.36
  255.8 8.9 %all-to-all-start.2 = ((f32[640,2,320]{0,2,1:T(8,128)}), f32[640,2,320]{0,2,1:T(8,128)}, u32[]{:S(2)}, u32[]{:S(2)}) async-start(f32[640,2,320]{0,2,1:T(8,128)} %bitcast.198), calls=%async_computation.2 | async-start | bytes 3276800 | tf_op jit(solution)/shard_map/all_to_all | solution.py:53
  264.6 6.9 copy-start.43
  264.6 6.9 copy-start.45
  264.6 6.9 copy-start.47
  264.7 14.2 %all-to-all-start.5 = ((bf16[640,2,320]{0,2,1:T(8,128)(2,1)}), bf16[640,2,320]{0,2,1:T(8,128)(2,1)S(1)}, u32[]{:S(2)}, u32[]{:S(2)}) async-start(bf16[640,2,320]{0,2,1:T(8,128)(2,1)} %bitcast.202), calls=%async_computation.5 | async-start | bytes 1638400 | tf_op jit(solution)/shard_map/all_to_all | solution.py:53
  271.6 4.1 copy-start.5
  278.9 7.3 all-to-all-start.4
  (33 other events, 85.7 us)
Sparse Core Ops, SparseCore 0:
  118.7 11.1 reduce-scatter.26
  146.2 11.1 reduce-scatter.22
  159.7 9.4 reduce-scatter.20
  171.9 10.2 reduce-scatter.24
  203.0 13.2 reduce-scatter.18
  218.4 13.0 reduce-scatter.32
  233.8 13.0 reduce-scatter.28
  253.9 128.0 all-reduce.6
  384.2 77.9 reduce-scatter.34
  467.0 124.7 reduce-scatter.36
  597.4 126.1 reduce-scatter.30
where the time goes:
time: 742 us; the launch traced here: 732 us
  waiting for transfers between devices  402 us (54%)
  matrix products  145 us (20%)
  local copies, waits for them, and re-layouts  58 us (8%)
  blocking collectives  44.6 us (6%)
  other arithmetic  38.3 us (5%)
  starting transfers between devices  27.4 us (4%)
  between operations  16.2 us (2%)
    unnamed x14, waiting for transfers between devices  252 us
    reduce_scatter x1, waiting for transfers between devices, per_device(): lax.psum_scatter(pair, 'dp', scatter_dimension=0, tiled=True)  130 us
    psum x1, blocking collectives, per_device(): lax.psum(jnp.concatenate([gain_local, shift_local], axis=0), ('dp', 'feat'))  40.8 us
    unnamed x141, local copies, waits for them, and re-layouts  30 us
    dot_general x7, matrix products, backward_product(): lax.dot_general(grad, weight, (((1,), (1,)), ((), ())), preferred_element...  28.6 us
    dot_general x7, matrix products, inner(): lax.dot_general(left, right, (((0,), (0,)), ((), ())), preferred_element_...  28.2 us
    dot_general x2, matrix products, attend_backward(): jnp.einsum('qhd,khd->hqk', grad_heads, split_heads(values), preferred_ele...  24.6 us
    reduce_scatter x7, waiting for transfers between devices, per_device(): lax.psum_scatter(term.astype(jnp.bfloat16), 'feat', scatter_dimension=1,...  19.4 us
  transfers between devices with their start and end apart: 17, of which 7 were waited for; matrix products, arithmetic and copies ran while one was open for 23% of the time, Pallas kernels for 0%

commit v1 on v0

--- a/solution.py
+++ b/solution.py
@@ -267,7 +267,9 @@
     input_grad = grad_mid_one + part_one
     gain_local = jnp.stack([gain_one, gain_two, gain_three], axis=0)
     shift_local = jnp.stack([shift_one, shift_two, shift_three], axis=0)
-    vectors = lax.psum(jnp.concatenate([gain_local, shift_local], axis=0), ("dp", "feat"))
+    vectors = jnp.sum(
+        lax.all_gather(jnp.concatenate([gain_local, shift_local], axis=0), ("dp", "feat")), axis=0
+    )
     half = vectors.shape[1] // lax.axis_size("feat")
     vectors = lax.dynamic_slice_in_dim(vectors, lax.axis_index("feat") * half, half, axis=1)
     gain_grad, shift_grad = (vectors[:3], vectors[3:])

time: 742 us -> 742 us (level)
    all_gather x0 -> x1, blocking collectives: none -> 43.9 us  [per_device(): lax.all_gather(jnp.concatenate([gain_local, shift_local], axis=0), ('dp',...]
    psum x1 -> x0, blocking collectives: 40.8 us -> none  [per_device(): lax.psum(jnp.concatenate([gain_local, shift_local], axis=0), ('dp', 'feat'))]
where the time goes in v1:
time: 742 us; the launch traced here: 732 us
  waiting for transfers between devices  399 us (54%)
  matrix products  145 us (20%)
  local copies, waits for them, and re-layouts  58 us (8%)
  blocking collectives  47.7 us (6%)
  other arithmetic  38.3 us (5%)
  starting transfers between devices  27.4 us (4%)
  between operations  16.2 us (2%)
    unnamed x14, waiting for transfers between devices  249 us
    reduce_scatter x1, waiting for transfers between devices, per_device(): lax.psum_scatter(pair, 'dp', scatter_dimension=0, tiled=True)  130 us
    all_gather x1, blocking collectives, per_device(): lax.all_gather(jnp.concatenate([gain_local, shift_local], axis=0), ('dp',...  43.9 us
    unnamed x141, local copies, waits for them, and re-layouts  30 us
    dot_general x7, matrix products, backward_product(): lax.dot_general(grad, weight, (((1,), (1,)), ((), ())), preferred_element...  28.6 us
    dot_general x7, matrix products, inner(): lax.dot_general(left, right, (((0,), (0,)), ((), ())), preferred_element_...  28.2 us
    dot_general x2, matrix products, attend_backward(): jnp.einsum('qhd,khd->hqk', grad_heads, split_heads(values), preferred_ele...  24.6 us
    reduce_scatter x7, waiting for transfers between devices, per_device(): lax.psum_scatter(term.astype(jnp.bfloat16), 'feat', scatter_dimension=1,...  19.4 us
  transfers between devices with their start and end apart: 17, of which 7 were waited for; matrix products, arithmetic and copies ran while one was open for 23% of the time, Pallas kernels for 0%

profile of v1, /device:TPU:0, one launch (start us, length us, event | category | flops | bytes accessed | tf_op | source)
XLA Modules:
  0.0 732.3 jit_solution(11777765707293187693)
XLA Ops:
  7.2 2.3 copy.193
  9.5 3.5 all-to-all-start.1
  20.5 2.7 copy.192
  23.2 4.7 all-to-all-start
  27.8 2.9 convolution_convert_fusion.6
  35.3 2.7 copy.191
  38.0 4.7 all-to-all-start.3
  58.6 8.8 %fusion.79 = f32[640,3072]{1,0:T(8,128)} fusion(bf16[640,640]{0,1:T(8,128)(2,1)S(1)} %fusion.60, bf16[3072,640]{1,0:T(8,128)(2,1)} %param.27), kind=kOutput, calls=%fused_computation.178 | convolution fusion | flops 2516582400 | bytes 12615680 | tf_op jit(solution)/shard_map/dot_general | solution.py:27
  68.6 2.5 fusion.77
  72.9 2.9 copy-done.1
  75.8 3.7 fusion.59
  79.5 2.8 fusion.73
  84.1 2.5 fusion.78
  88.7 2.7 copy-done.2
  91.4 3.8 fusion.58
  97.4 12.5 %fusion.7 = (bf16[640,3072]{1,0:T(8,128)(2,1)S(1)}, bf16[640,3072]{1,0:T(8,128)(2,1)}) fusion(f32[640,3072]{1,0:T(8,128)} %fusion.79, bf16[640,3072]{1,0:T(8,128)(2,1)S(1)} %copy-done.50, f32[640,640]{0,1:T(8,128)S(1)} %get-tuple-element.118, f32[640]{0:T(1024)S(1)} %get-tuple-element.91, f32[640]{0:T(1024)S(1)} %get-tuple-element.130, ...), kind=kOutput, calls=%fused_computation.24 | convolution fusion | flops 2561884160 | bytes 21309440 | tf_op jit(solution)/shard_map/dot_general | solution.py:218
  109.9 3.6 fusion.44
  118.6 2.6 convolution_convert_fusion.11
  121.3 12.5 %multiply_reduce_fusion.1 = (f32[8,640]{1,0:T(8,128)S(1)}, f32[8,640,640]{1,2,0:T(8,128)}) fusion(f32[8,640,640]{1,2,0:T(8,128)} %copy-done.2, f32[8,640]{1,0:T(8,128)S(1)} %log_add_fusion.1, bf16[640,8,80]{0,2,1:T(8,128)(2,1)S(1)} %bitcast.173, bf16[640,8,80]{0,2,1:T(8,128)(2,1)} %bitcast.187), kind=kOutput, calls=%fused_computation.9 | convolution fusion | flops 534113280 | bytes 27893760 | tf_op jit(solution)/shard_map/qhd,khd->hqk/dot_general | solution.py:121
  133.8 6.6 multiply_convert_fusion.1
  146.4 3.2 fusion.45
  153.2 5.6 multiply_convert_fusion.2
  158.8 7.3 fusion.52
  167.0 2.8 fusion.22
  170.1 2.4 convolution_convert_fusion.9
  172.5 12.1 %multiply_reduce_fusion = (f32[8,640]{1,0:T(8,128)S(1)}, f32[8,640,640]{1,2,0:T(8,128)}) fusion(f32[8,640,640]{1,2,0:T(8,128)} %copy-done.1, f32[8,640]{1,0:T(8,128)S(1)} %log_add_fusion, bf16[640,8,80]{0,2,1:T(8,128)(2,1)S(1)} %bitcast.175, bf16[640,8,80]{0,2,1:T(8,128)(2,1)S(1)} %bitcast.185), kind=kOutput, calls=%fused_computation.6 | convolution fusion | flops 534113280 | bytes 27893760 | tf_op jit(solution)/shard_map/qhd,khd->hqk/dot_general | solution.py:121
  185.6 6.6 multiply_convert_fusion
  198.9 3.9 convolution_convert_fusion.3
  204.0 7.4 %convolution_convert_fusion = bf16[3072,640]{0,1:T(8,128)(2,1)} fusion(bf16[640,640]{0,1:T(8,128)(2,1)S(1)} %copy-done.34, bf16[640,3072]{1,0:T(8,128)(2,1)} %get-tuple-element.120), kind=kOutput, calls=%fused_computation.37 | convolution fusion | flops 2538209280 | bytes 8683520 | tf_op jit(solution)/shard_map/dot_general | solution.py:21
  211.5 8.4 %convolution_convert_fusion.1 = bf16[640,3072]{1,0:T(8,128)(2,1)} fusion(bf16[640,3072]{1,0:T(8,128)(2,1)} %copy-done.55, f32[640,640]{0,1:T(8,128)} %copy-done.18, f32[640]{0:T(1024)S(1)} %get-tuple-element.91, f32[640]{0:T(1024)S(1)} %get-tuple-element.130, f32[640]{0:T(1024)S(1)} %get-tuple-element.108, f32[640]{0:T(1024)S(1)} %get-tuple-element.107), kind=kOutput, calls=%fused_computation.38 | convolution fusion | flops 2520596480 | bytes 9512960 | tf_op jit(solution)/shard_map/dot_general | solution.py:21
  220.7 2.5 copy.170
  223.4 8.2 %reduce-scatter.33.cloned.1.call-done = bf16[3072,320]{0,1:T(8,128)(2,1)} async-done(((bf16[3072,640]{0,1:T(8,128)(2,1)}), bf16[3072,320]{0,1:T(8,128)(2,1)}) %reduce-scatter.33.cloned.1.call-update) | async-done | bytes 1966096 | tf_op jit(solution)/shard_map/reduce_scatter | solution.py:287
  231.6 4.1 copy.180
  235.8 11.1 %reduce-scatter.29.cloned.1.call-done = bf16[640,1536]{1,0:T(8,128)(2,1)} async-done(((bf16[640,3072]{1,0:T(8,128)(2,1)}), bf16[640,1536]{1,0:T(8,128)(2,1)}) %reduce-scatter.29.cloned.1.call-update) | async-done | bytes 1966096 | tf_op jit(solution)/shard_map/reduce_scatter | solution.py:287
  246.9 8.8 %convert_add_fusion.1 = f32[640,640]{0,1:T(8,128)} fusion(f32[640,640]{0,1:T(8,128)} %copy-done.18, bf16[3072,640]{1,0:T(8,128)(2,1)} %param.27, f32[640]{0:T(1024)S(1)} %fusion.61, bf16[640,3072]{1,0:T(8,128)(2,1)} %get-tuple-element.120), kind=kOutput, calls=%fused_computation.93 | convolution fusion | flops 2537881600 | bytes 11143680 | tf_op jit(solution)/shard_map/dot_general | solution.py:221
  255.8 4.8 all-to-all-start.2
  260.6 4.1 convolution_convert_fusion.7
  264.7 4.0 all-to-all-start.5
  268.7 2.9 copy.185
  271.6 4.0 fusion.46
  275.7 3.2 fusion.34
  278.9 4.7 all-to-all-start.4
  286.2 2.7 copy.186
  289.0 43.9 %all-gather.3 = f32[32,6,640]{2,1,0:T(8,128)S(1)} all-gather(f32[1,6,640]{2,1,0:T(8,128)S(1)} %bitcast.212), channel_id=2, replica_groups=mesh['dp'=16,'feat'=2] {'dp','feat'}, dimensions={0}, use_global_device_ids=true | all-gather | bytes 506880 | tf_op jit(solution)/shard_map/all_gather | solution.py:271
  334.9 47.1 %all-reduce.7.cloned.1.call-done = (bf16[640,320]{0,1:T(8,128)(2,1)}, bf16[640,320]{0,1:T(8,128)(2,1)}, bf16[640,640]{0,1:T(8,128)(2,1)}, bf16[640,320]{0,1:T(8,128)(2,1)}) async-done(((bf16[640,320]{0,1:T(8,128)(2,1)}, bf16[640,320]{0,1:T(8,128)(2,1)}, bf16[640,640]{0,1:T(8,128)(2,1)}, bf16[640,320]{0,1:T(8,128)(2,1)}), (bf16[640,320]{0,1:T(8,128)(2,1)}, bf16[640,320]{0,1:T(8,128)(2,1)}, ...) | async-done | bytes 2048016
  389.1 73.2 %reduce-scatter.35.cloned.1.call-done = bf16[40,960]{1,0:T(8,128)(2,1)} async-done(((bf16[640,960]{1,0:T(8,128)(2,1)}), bf16[40,960]{1,0:T(8,128)(2,1)}) %reduce-scatter.35.cloned.1.call-update) | async-done | bytes 76816
  464.2 127.7 %reduce-scatter.37.cloned.1.call-done = bf16[192,320]{1,0:T(8,128)(2,1)} async-done(((bf16[3072,320]{1,0:T(8,128)(2,1)}), bf16[192,320]{1,0:T(8,128)(2,1)}) %reduce-scatter.37.cloned.1.call-update) | async-done | bytes 122896
  593.7 129.9 %reduce-scatter.31.cloned.1.call-done = bf16[40,1536]{1,0:T(8,128)(2,1)} async-done(((bf16[640,1536]{1,0:T(8,128)(2,1)}), bf16[40,1536]{1,0:T(8,128)(2,1)}) %reduce-scatter.31.cloned.1.call-update) | async-done | bytes 122896 | tf_op jit(solution)/shard_map/reduce_scatter | solution.py:289
  (238 shorter events, 78.5 us)
Async XLA Ops:
  7.2 40.5 %copy-start = (bf16[640,1920]{1,0:T(8,128)(2,1)S(1)}, bf16[640,1920]{1,0:T(8,128)(2,1)}, u32[]{:S(2)}) copy-start(bf16[640,1920]{1,0:T(8,128)(2,1)} %param.21) | copy-start | bytes 7372804
  7.2 5.8 copy-start.52
  7.2 7.8 %copy-start.53 = (s32[1,24]{1,0:T(1,128)S(1)}, s32[1,24]{1,0:T(1,128)}, u32[]{:S(2)}) copy-start(s32[1,24]{1,0:T(1,128)} %param.18) | copy-start | bytes 292
  7.2 9.3 %copy-start.48 = (f32[3,320]{1,0:T(4,128)S(1)}, f32[3,320]{1,0:T(4,128)}, u32[]{:S(2)}) copy-start(f32[3,320]{1,0:T(4,128)} %param.19) | copy-start | bytes 11524
  7.2 11.3 %copy-start.49 = (f32[3,320]{1,0:T(4,128)S(1)}, f32[3,320]{1,0:T(4,128)}, u32[]{:S(2)}) copy-start(f32[3,320]{1,0:T(4,128)} %param.20) | copy-start | bytes 11524
  9.5 13.7 %all-to-all-start.1 = ((bf16[2,640,320]{1,2,0:T(8,128)(2,1)}), bf16[2,640,320]{1,2,0:T(8,128)(2,1)S(1)}, u32[]{:S(2)}, u32[]{:S(2)}) async-start(bf16[2,640,320]{1,2,0:T(8,128)(2,1)} %bitcast.162), calls=%async_computation.1 | async-start | bytes 1638400 | tf_op jit(solution)/shard_map/all_to_all | solution.py:49
  23.2 4.7 copy-start.29
  23.2 14.9 %all-to-all-start = ((f32[2,640,320]{1,2,0:T(8,128)}), f32[2,640,320]{1,2,0:T(8,128)}, u32[]{:S(2)}, u32[]{:S(2)}) async-start(f32[2,640,320]{1,2,0:T(8,128)} %bitcast.178), calls=%async_computation | async-start | bytes 3276800 | tf_op jit(solution)/shard_map/all_to_all | solution.py:49
  38.0 8.0 %copy-start.42 = (f32[640]{0:T(1024)}, f32[640]{0:T(1024)S(1)}, u32[]{:S(2)}) copy-start(f32[640]{0:T(1024)S(1)} %get-tuple-element.128) | copy-start | bytes 7684
  38.0 19.0 %all-to-all-start.3 = ((f32[2,640,320]{1,2,0:T(8,128)}), f32[2,640,320]{1,2,0:T(8,128)}, u32[]{:S(2)}, u32[]{:S(2)}) async-start(f32[2,640,320]{1,2,0:T(8,128)} %bitcast.177), calls=%async_computation.3 | async-start | bytes 3276800 | tf_op jit(solution)/shard_map/all_to_all | solution.py:49
  42.7 177.3 %reduce-scatter.27.cloned.1.call-start = ((), (), s32[]{:S(2)}) async-start(), calls=%async_computation.20 | async-start | bytes 1228800 | tf_op jit(solution)/shard_map/reduce_scatter | solution.py:287
  58.6 8.8 %copy-start.33 = (bf16[640,640]{0,1:T(8,128)(2,1)}, bf16[640,640]{0,1:T(8,128)(2,1)S(1)}, u32[]{:S(2)}) copy-start(bf16[640,640]{0,1:T(8,128)(2,1)S(1)} %fusion.60) | copy-start | bytes 2457604
  58.6 10.0 %copy-start.12 = (bf16[640,640]{0,1:T(8,128)(2,1)S(1)}, bf16[640,640]{0,1:T(8,128)(2,1)}, u32[]{:S(2)}) copy-start(bf16[640,640]{0,1:T(8,128)(2,1)} %copy.140) | copy-start | bytes 2457604
  58.6 10.0 %copy-start.16 = (bf16[640,640]{0,1:T(8,128)(2,1)S(1)}, bf16[640,640]{0,1:T(8,128)(2,1)}, u32[]{:S(2)}) copy-start(bf16[640,640]{0,1:T(8,128)(2,1)} %copy.139) | copy-start | bytes 2457604
  71.1 4.7 copy-start.1
  86.7 4.7 copy-start.2
  96.4 17.2 %copy-start.18 = (f32[640,640]{0,1:T(8,128)}, f32[640,640]{0,1:T(8,128)S(1)}, u32[]{:S(2)}) copy-start(f32[640,640]{0,1:T(8,128)S(1)} %get-tuple-element.118) | copy-start | bytes 4915204
  118.6 101.5 %reduce-scatter.23.cloned.1.call-start = ((), (), s32[]{:S(2)}) async-start(), calls=%async_computation.18 | async-start | bytes 1228800 | tf_op jit(solution)/shard_map/reduce_scatter | solution.py:287
  121.2 12.6 %slice-start.4 = ((s8[13107200]{0:T(1024)(128)(4,1)}), s8[4194304]{0:T(1024)(128)(4,1)S(1)}, s32[]{:S(2)}) async-start(s8[13107200]{0:T(1024)(128)(4,1)} %bitcast.165), calls=%async_computation.31 | async-start | bytes 8388608
  121.2 12.5 %slice-start.5 = ((s8[13107200]{0:T(1024)(128)(4,1)}), s8[4194304]{0:T(1024)(128)(4,1)S(1)}, s32[]{:S(2)}) async-start(s8[13107200]{0:T(1024)(128)(4,1)} %bitcast.165), calls=%async_computation.32 | async-start | bytes 8388608
  121.2 12.5 %slice-start.6 = ((s8[13107200]{0:T(1024)(128)(4,1)}), s8[4194304]{0:T(1024)(128)(4,1)S(1)}, s32[]{:S(2)}) async-start(s8[13107200]{0:T(1024)(128)(4,1)} %bitcast.165), calls=%async_computation.33 | async-start | bytes 8388608
  121.2 12.5 %slice-start.7 = ((s8[13107200]{0:T(1024)(128)(4,1)}), s8[524288]{0:T(1024)(128)(4,1)S(1)}, s32[]{:S(2)}) async-start(s8[13107200]{0:T(1024)(128)(4,1)} %bitcast.165), calls=%async_computation.34 | async-start | bytes 1048576
  133.8 6.6 copy-start.15
  146.1 73.9 %reduce-scatter.21.cloned.1.call-start = ((), (), s32[]{:S(2)}) async-start(), calls=%async_computation.17 | async-start | bytes 1228800 | tf_op jit(solution)/shard_map/reduce_scatter | solution.py:287
  153.1 66.9 %reduce-scatter.25.cloned.1.call-start = ((), (), s32[]{:S(2)}) async-start(), calls=%async_computation.19 | async-start | bytes 2457600 | tf_op jit(solution)/shard_map/reduce_scatter | solution.py:287
  158.8 7.3 copy-start.35
  158.8 8.2 %copy-start.30 = (bf16[2,640,320]{1,2,0:T(8,128)(2,1)S(1)}, bf16[2,640,320]{1,2,0:T(8,128)(2,1)}, u32[]{:S(2)}) copy-start(bf16[2,640,320]{1,2,0:T(8,128)(2,1)} %copy-done.29) | copy-start | bytes 2457604
  169.8 51.0 %reduce-scatter.19.cloned.1.call-start = ((), (), s32[]{:S(2)}) async-start(), calls=%async_computation.16 | async-start | bytes 3686400 | tf_op jit(solution)/shard_map/reduce_scatter | solution.py:287
  172.5 12.1 %slice-start = ((s8[13107200]{0:T(1024)(128)(4,1)}), s8[4194304]{0:T(1024)(128)(4,1)S(1)}, s32[]{:S(2)}) async-start(s8[13107200]{0:T(1024)(128)(4,1)} %bitcast.163), calls=%async_computation.27 | async-start | bytes 8388608
  172.5 12.1 %slice-start.1 = ((s8[13107200]{0:T(1024)(128)(4,1)}), s8[4194304]{0:T(1024)(128)(4,1)S(1)}, s32[]{:S(2)}) async-start(s8[13107200]{0:T(1024)(128)(4,1)} %bitcast.163), calls=%async_computation.28 | async-start | bytes 8388608
  172.5 12.9 %slice-start.2 = ((s8[13107200]{0:T(1024)(128)(4,1)}), s8[4194304]{0:T(1024)(128)(4,1)S(1)}, s32[]{:S(2)}) async-start(s8[13107200]{0:T(1024)(128)(4,1)} %bitcast.163), calls=%async_computation.29 | async-start | bytes 8388608
  172.5 13.1 %slice-start.3 = ((s8[13107200]{0:T(1024)(128)(4,1)}), s8[524288]{0:T(1024)(128)(4,1)S(1)}, s32[]{:S(2)}) async-start(s8[13107200]{0:T(1024)(128)(4,1)} %bitcast.163), calls=%async_computation.30 | async-start | bytes 1048576
  185.6 6.6 copy-start.17
  202.8 28.7 %reduce-scatter.33.cloned.1.call-start = ((), (), s32[]{:S(2)}) async-start(), calls=%async_computation.23 | async-start | bytes 5898240 | tf_op jit(solution)/shard_map/reduce_scatter | solution.py:287
  211.4 35.5 %reduce-scatter.29.cloned.1.call-start = ((), (), s32[]{:S(2)}) async-start(), calls=%async_computation.21 | async-start | bytes 5898240 | tf_op jit(solution)/shard_map/reduce_scatter | solution.py:287
  219.9 162.1 %all-reduce.7.cloned.1.call-start = ((), (), s32[]{:S(2)}) async-start(), calls=%async_computation.26 | async-start | bytes 4096000
  220.7 241.6 %reduce-scatter.35.cloned.1.call-start = ((), (), s32[]{:S(2)}) async-start(), calls=%async_computation.24 | async-start | bytes 1392640
  223.3 368.6 %reduce-scatter.37.cloned.1.call-start = ((), (), s32[]{:S(2)}) async-start(), calls=%async_computation.25 | async-start | bytes 2506752
  235.7 487.9 %reduce-scatter.31.cloned.1.call-start = ((), (), s32[]{:S(2)}) async-start(), calls=%async_computation.22 | async-start | bytes 2088960 | tf_op jit(solution)/shard_map/reduce_scatter | solution.py:289
  255.8 4.8 copy-start.36
  255.8 8.9 %all-to-all-start.2 = ((f32[640,2,320]{0,2,1:T(8,128)}), f32[640,2,320]{0,2,1:T(8,128)}, u32[]{:S(2)}, u32[]{:S(2)}) async-start(f32[640,2,320]{0,2,1:T(8,128)} %bitcast.199), calls=%async_computation.2 | async-start | bytes 3276800 | tf_op jit(solution)/shard_map/all_to_all | solution.py:53
  264.6 6.9 copy-start.43
  264.6 6.9 copy-start.45
  264.6 6.9 copy-start.47
  264.7 14.2 %all-to-all-start.5 = ((bf16[640,2,320]{0,2,1:T(8,128)(2,1)}), bf16[640,2,320]{0,2,1:T(8,128)(2,1)S(1)}, u32[]{:S(2)}, u32[]{:S(2)}) async-start(bf16[640,2,320]{0,2,1:T(8,128)(2,1)} %bitcast.203), calls=%async_computation.5 | async-start | bytes 1638400 | tf_op jit(solution)/shard_map/all_to_all | solution.py:53
  271.6 4.1 copy-start.5
  278.9 7.3 all-to-all-start.4
  285.0 48.0 %copy-start.54 = (u32[32]{0:T(128)S(1)}, u32[32]{0:T(128)}, u32[]{:S(2)}) copy-start(u32[32]{0:T(128)} %constant.54) | copy-start | bytes 388
  (33 other events, 85.7 us)
Sparse Core Ops, SparseCore 0:
  118.7 11.1 reduce-scatter.26
  146.2 11.1 reduce-scatter.22
  159.7 9.4 reduce-scatter.20
  171.9 10.2 reduce-scatter.24
  203.0 13.2 reduce-scatter.18
  218.4 13.0 reduce-scatter.32
  233.8 13.0 reduce-scatter.28
  253.9 128.1 all-reduce.6
  384.3 77.9 reduce-scatter.34
  467.1 124.7 reduce-scatter.36
  597.5 126.1 reduce-scatter.30
